TPU v7x, 512 devices: a whole 4x4x16 slice. The times are simulated.
512 devices in a mesh: row: 16 (over x, y_lo, core), col: 32 (over z, y_hi).
Axes of the slice: x: 4, y: 4 (y_hi: 2, y_lo: 2; y = y_hi * 2 + y_lo), z: 16, core: 2. Of those that a mesh axis runs over, the one named last changes fastest.
Arguments:
- momentum: bfloat16 [3584, 18432], P('row', 'col'), may hold values from -0.020446655 to 0.020446655
Outputs:
- update: bfloat16 [3584, 18432], P('row', 'col')
All inputs are finite; a program needn't handle non-finite values.
Results may differ from a plain program's by a relative error of at most 0.0054.
Values may be sent and summed in bfloat16 or wider, within the bound.
A program may use at most 64 MiB of HBM per device.

v0:
```python
import math

import jax
import jax.numpy as jnp
from jax import lax
from jax.sharding import PartitionSpec as P

M = 3584
N = 18432


coef_linear = 3.4445
coef_quad = -4.775
coef_cubic = 2.0315


def rows_product(left, right):
    return lax.dot_general(
        left, right, (((1,), (1,)), ((), ())), preferred_element_type=jnp.float32
    )


def body(momentum):
    panel = lax.all_gather(momentum, "row", axis=0, tiled=True)
    term = rows_product(momentum, panel)
    own = lax.psum_scatter(term, "col", scatter_dimension=1, tiled=True).astype(jnp.bfloat16)
    gram_rows = lax.all_gather(own, "col", axis=1, tiled=True)
    block = gram_rows
    square = jnp.dot(
        block, lax.all_gather(own, "row", axis=0, tiled=True), preferred_element_type=jnp.float32
    )
    poly = (coef_quad * own.astype(jnp.float32) + coef_cubic * square).astype(jnp.bfloat16)
    block = panel
    product = jnp.dot(
        lax.all_gather(poly, "col", axis=1, tiled=True), block, preferred_element_type=jnp.float32
    )
    factor = math.sqrt(max(M, N))
    return ((coef_linear * momentum.astype(jnp.float32) + product) * factor).astype(jnp.bfloat16)


def solution(mesh):
    return jax.shard_map(
        body,
        mesh=mesh,
        in_specs=(P("row", "col"),),
        out_specs=P("row", "col"),
        check_vma=False,
    )
```

profile of v0, /device:TPU:1, one launch (start us, length us, event | category | flops | bytes accessed | tf_op | source)
XLA Modules:
  0.0 1045.3 jit_solution(464357451757110636)
XLA Ops:
  6.5 0.0 all-gather.4.cloned.1.call-start
  6.5 0.7 all-gather.4.cloned.1.call-update
  7.3 0.0 reduce-scatter.4.cloned.1.call-start
  7.3 53.6 %all-gather.4.cloned.1.call-done = bf16[3584,576]{1,0:T(8,128)(2,1)} async-done(((bf16[224,576]{1,0:T(8,128)(2,1)}), bf16[3584,576]{1,0:T(8,128)(2,1)}) %all-gather.4.cloned.1.call-update) | async-done | bytes 4128784 | tf_op jit(solution)/shard_map/all_gather | solution.py:24
  60.9 5.8 convolution_bitcast_fusion
  66.7 0.0 copy-start
  66.7 0.0 reduce-scatter.4.cloned.1.call-update
  66.8 0.0 all-gather.6.cloned.1.call-start
  66.8 670.4 %reduce-scatter.4.cloned.1.call-done = f32[112,224]{1,0:T(8,128)} async-done(((f32[3584,224]{1,0:T(8,128)}), f32[112,224]{1,0:T(8,128)}) %reduce-scatter.4.cloned.1.call-update) | async-done | bytes 100368
  737.2 1.0 copy.5
  738.2 0.7 copy.2
  738.9 0.0 all-gather.6.cloned.1.call-update
  739.0 0.0 all-gather.8.cloned.1.call-start
  739.0 32.0 %all_gather.14 = bf16[3584,112]{1,0:T(8,128)(2,1)S(1)} all-gather(bf16[224,112]{1,0:T(8,128)(2,1)S(1)} %copy.5), channel_id=1, replica_groups=mesh['row'=16,'col'=32] {'row'}, dimensions={0}, use_global_device_ids=true | all-gather | bytes 852992 | tf_op jit(solution)/shard_map/all_gather | solution.py:30
  771.0 116.5 %all-gather.6.cloned.1.call-done = bf16[224,3584]{0,1:T(8,128)(2,1)} async-done(((bf16[224,112]{0,1:T(8,128)(2,1)}), bf16[224,3584]{0,1:T(8,128)(2,1)}) %all-gather.6.cloned.1.call-update) | async-done | bytes 1605648 | tf_op jit(solution)/shard_map/all_gather | solution.py:27
  887.5 2.2 fusion.3
  889.7 0.7 copy.3
  890.4 0.0 all-gather.8.cloned.1.call-update
  890.4 143.3 %all-gather.8.cloned.1.call-done = bf16[224,3584]{0,1:T(8,128)(2,1)} async-done(((bf16[224,112]{0,1:T(8,128)(2,1)}), bf16[224,3584]{0,1:T(8,128)(2,1)}) %all-gather.8.cloned.1.call-update) | async-done | bytes 1605648 | tf_op jit(solution)/shard_map/all_gather | solution.py:35
  1033.8 0.0 copy-done
  1033.8 5.0 fusion.1
Async XLA Ops:
  6.5 54.4 %all-gather.4.cloned.1.call-start = ((), (), s32[]{:S(2)}) async-start(), calls=%async_computation.1 | async-start | bytes 4874240 | tf_op jit(solution)/shard_map/all_gather | solution.py:24
  7.3 729.9 %reduce-scatter.4.cloned.1.call-start = ((), (), s32[]{:S(2)}) async-start(), calls=%async_computation.4 | async-start | bytes 3784704
  66.7 967.0 %copy-start = (bf16[224,576]{1,0:T(8,128)(2,1)S(1)}, bf16[224,576]{1,0:T(8,128)(2,1)}, u32[]{:S(2)}) copy-start(bf16[224,576]{1,0:T(8,128)(2,1)} %param.1) | copy-start | bytes 774148
  66.8 820.7 %all-gather.6.cloned.1.call-start = ((), (), s32[]{:S(2)}) async-start(), calls=%async_computation.2 | async-start | bytes 1892352 | tf_op jit(solution)/shard_map/all_gather | solution.py:27
  739.0 294.8 %all-gather.8.cloned.1.call-start = ((), (), s32[]{:S(2)}) async-start(), calls=%async_computation.3 | async-start | bytes 1892352 | tf_op jit(solution)/shard_map/all_gather | solution.py:35
Sparse Core Ops, SparseCore 0:
  9.5 51.3 all-gather.3
  66.9 670.2 reduce-scatter.3
  740.8 146.6 all-gather.5
  890.9 142.8 all-gather.7
where the time goes:
time: 1050 us
  waiting for transfers between devices  985 us (94%)
  blocking collectives  32 us (3%)
  between operations  13.1 us (1%)
  matrix products  13 us (1%)
    unnamed x5, waiting for transfers between devices  671 us
    all_gather x1, waiting for transfers between devices, body(): lax.all_gather(poly, 'col', axis=1, tiled=True)  143 us
    all_gather x1, waiting for transfers between devices, body(): gram_rows = lax.all_gather(own, 'col', axis=1, tiled=True)  116 us
    all_gather x1, waiting for transfers between devices, body(): panel = lax.all_gather(momentum, 'row', axis=0, tiled=True)  53.6 us
    all_gather x1, blocking collectives, body(): lax.all_gather(own, 'row', axis=0, tiled=True)  32 us
  transfers between devices with their start and end apart: 4, of which 4 were waited for; matrix products, arithmetic and copies ran while one was open for 0% of the time, Pallas kernels for 0%

commit v1 on v0

v1 whole, which is shorter than its diff:
```python
import functools
import math

import jax
import jax.numpy as jnp
from jax import lax
from jax.experimental import pallas as pl
from jax.experimental.pallas import tpu as pltpu
from jax.sharding import PartitionSpec as P

M = 3584
N = 18432

coef_linear = 3.4445
coef_quad = -4.775
coef_cubic = 2.0315

SIDE = 4
DEPTH = 16
BLOCK = M // SIDE
ROWS = BLOCK // SIDE
COLS = N // 32
HALF = BLOCK // 2
CHUNK = 32
USED = HALF // CHUNK
NT = (((1,), (1,)), ((), ()))


def kernel(
    stop, m_ref, out_ref, xi, xj, acc, sib_out, sib_in, plus_out, plus_in, minus_out, minus_in,
    gram, gram_t, t_out, t_in, u, p_out, p_in,
    x_send, x_recv, s_send, s_recv, rs_send, rs_recv, ag_send, ag_recv, f_send, f_recv,
    t_send, t_recv, u_send, u_recv, p_send, p_recv,
):
    row, col = lax.axis_index("row"), lax.axis_index("col")
    x, y_lo, c = row // 4, (row // 2) % 2, row % 2
    z, y_hi = col // 2, col % 2
    y = y_hi * 2 + y_lo
    quarter = y_lo * 2 + c

    def device(x_, y_hi_, y_lo_, z_, c_):
        return ((x_ * 2 + y_lo_) * 2 + c_, z_ * 2 + y_hi_)

    def at(x_, y_, c_):
        return device(x_, y_ // 2, y_ % 2, z, c_)

    def remote(src, dst, send, recv, where):
        return pltpu.make_async_remote_copy(
            src_ref=src, dst_ref=dst, send_sem=send, recv_sem=recv,
            device_id=where, device_id_type=pl.DeviceIdType.MESH,
        )

    def arrived(dst, recv):
        pltpu.make_async_copy(dst, dst, recv).wait()

    sibling = at(x, y, 1 - c)
    right = device(x, y_hi, y_lo, (z + 1) % DEPTH, c)
    left = device(x, y_hi, y_lo, (z + DEPTH - 1) % DEPTH, c)
    own_i = c == y_hi
    own_j = jnp.logical_and(own_i, x == y)

    barrier = pltpu.get_barrier_semaphore()

    def signal(where):
        pl.semaphore_signal(barrier, inc=1, device_id=where, device_id_type=pl.DeviceIdType.MESH)

    def to_i(k):
        return at(x, k, y_hi)

    def from_i(k):
        return at(x, c * 2 + k // 2, k % 2)

    def to_j(k):
        return at(k, x, y_hi)

    def from_j(k):
        return at(y, c * 2 + k // 2, k % 2)

    signal(sibling)
    signal(right)
    signal(left)
    for k in range(SIDE):
        self_i = jnp.logical_and(own_i, y == k)

        @pl.when(jnp.logical_not(self_i))
        def _():
            signal(to_i(k))

        @pl.when(jnp.logical_not(jnp.logical_and(own_i, quarter == k)))
        def _():
            signal(from_i(k))

        @pl.when(jnp.logical_not(jnp.logical_and(own_j, x == k)))
        def _():
            signal(to_j(k))

        @pl.when(jnp.logical_not(jnp.logical_and(own_j, quarter == k)))
        def _():
            signal(from_j(k))

        if k:
            signal(at((x + k) % SIDE, y, c))
    count = 3 + 4 * SIDE + SIDE - 1
    pl.semaphore_wait(
        barrier, count - 2 * own_i.astype(jnp.int32) - 2 * own_j.astype(jnp.int32)
    )

    def x_copies(k):
        to_a = (y + 1 + k) % SIDE
        to_b = (x + 1 + k) % SIDE
        a = (m_ref, xi.at[quarter], x_send.at[0, k], x_recv.at[0, quarter])
        b = (m_ref, xj.at[quarter], x_send.at[1, k], x_recv.at[1, quarter])
        return (
            (a, to_i(to_a), jnp.logical_and(own_i, k == SIDE - 1)),
            (b, to_j(to_b), jnp.logical_and(own_j, k == SIDE - 1)),
        )

    for k in range(SIDE):
        for (src, dst, send, recv), where, local in x_copies(k):

            @pl.when(local)
            def _():
                pltpu.make_async_copy(src, dst, recv).start()

            @pl.when(jnp.logical_not(local))
            def _():
                remote(src, dst, send, recv, where).start()

    acc[USED:] = jnp.zeros_like(acc[USED:])
    for k in range(SIDE):
        arrived(xi.at[k], x_recv.at[0, k])
        arrived(xj.at[k], x_recv.at[1, k])

    def finish_x():
        for k in range(SIDE):
            for (src, dst, send, recv), where, local in x_copies(k):

                @pl.when(jnp.logical_not(local))
                def _():
                    remote(src, dst, send, recv, where).wait_send()

    if stop == 1:
        finish_x()
        out_ref[...] = xi[0] + xj[0]
        return

    xi_all = xi[...].reshape(BLOCK, COLS)
    for k in range(2):
        part = lax.dot_general(
            xj[(1 - c) * 2 + k], xi_all, NT, preferred_element_type=jnp.float32
        )
        sib_out[k] = part.astype(jnp.bfloat16)
        remote(sib_out.at[k], sib_in.at[k], s_send.at[k], s_recv.at[k], sibling).start()
    for k in range(2):
        part = lax.dot_general(xj[c * 2 + k], xi_all, NT, preferred_element_type=jnp.float32)
        acc[k * 7 : (k + 1) * 7] = part.reshape(7, CHUNK, BLOCK)
    for k in range(2):
        remote(sib_out.at[k], sib_in.at[k], s_send.at[k], s_recv.at[k], sibling).wait()
        acc[k * 7 : (k + 1) * 7] += sib_in[k].reshape(7, CHUNK, BLOCK).astype(jnp.float32)

    if stop == 2:
        finish_x()
        out_ref[...] = acc[0:7].reshape(ROWS, BLOCK)[:, :COLS].astype(jnp.bfloat16)
        return

    def plus(s):
        return remote(plus_out.at[s], plus_in.at[s], rs_send.at[0, s], rs_recv.at[0, s], right)

    def minus(s):
        return remote(minus_out.at[s], minus_in.at[s], rs_send.at[1, s], rs_recv.at[1, s], left)

    plus_out[0] = acc[(z + 8) % DEPTH].astype(jnp.bfloat16)
    plus(0).start()
    minus_out[0] = acc[(z + DEPTH - 7) % DEPTH].astype(jnp.bfloat16)
    minus(0).start()

    def rs_plus(s):
        plus(s - 1).wait_recv()
        o = (z + 8 - s) % DEPTH
        plus_out[s] = (acc[o] + plus_in[s - 1].astype(jnp.float32)).astype(jnp.bfloat16)
        plus(s).start()

    def rs_minus(s):
        minus(s - 1).wait_recv()
        o = (z + DEPTH - 7 + s) % DEPTH
        minus_out[s] = (acc[o] + minus_in[s - 1].astype(jnp.float32)).astype(jnp.bfloat16)
        minus(s).start()

    @pl.loop(1, 7)
    def _(s):
        rs_plus(s)
        rs_minus(s)

    rs_plus(7)
    minus(6).wait_recv()
    plus(7).wait_recv()

    def slot(core, o):
        return jnp.where(o < USED, core * USED + o, 2 * USED + core * 2 + o - USED)

    total = acc[z] + plus_in[7].astype(jnp.float32) + minus_in[6].astype(jnp.float32)
    gram[slot(c, z)] = total.astype(jnp.bfloat16)

    def finish_rs():
        @pl.loop(0, 7)
        def _(s):
            plus(s).wait_send()
            minus(s).wait_send()

        plus(7).wait_send()

    if stop == 3:
        finish_x()
        finish_rs()
        out_ref[0:32] = gram[slot(c, z)][:, :COLS]
        return

    def ag_plus(s):
        k = slot(c, (z + DEPTH - s) % DEPTH)
        return remote(gram.at[k], gram.at[k], ag_send.at[0, s], ag_recv.at[0, s], right)

    def ag_minus(s):
        k = slot(c, (z + s) % DEPTH)
        return remote(gram.at[k], gram.at[k], ag_send.at[1, s], ag_recv.at[1, s], left)

    def ag_plus_in(s):
        arrived(gram.at[slot(c, (z + DEPTH - 1 - s) % DEPTH)], ag_recv.at[0, s])

    def ag_minus_in(s):
        arrived(gram.at[slot(c, (z + 1 + s) % DEPTH)], ag_recv.at[1, s])

    def hand(o):
        k = slot(c, o)
        return remote(gram.at[k], gram.at[k], f_send.at[o], f_recv.at[o], sibling)

    ag_plus(0).start()
    ag_minus(0).start()
    hand(z).start()

    @pl.loop(1, 7)
    def _(s):
        ag_plus_in(s - 1)
        ag_plus(s).start()
        hand((z + DEPTH - s) % DEPTH).start()
        ag_minus_in(s - 1)
        ag_minus(s).start()
        hand((z + s) % DEPTH).start()

    ag_plus_in(6)
    ag_plus(7).start()
    hand((z + DEPTH - 7) % DEPTH).start()
    ag_minus_in(6)
    hand((z + 7) % DEPTH).start()
    ag_plus_in(7)
    hand((z + 8) % DEPTH).start()

    @pl.loop(0, DEPTH)
    def _(o):
        arrived(gram.at[slot(1 - c, o)], f_recv.at[o])

    def finish_ag():
        @pl.loop(0, 7)
        def _(s):
            ag_plus(s).wait_send()
            ag_minus(s).wait_send()

        ag_plus(7).wait_send()

        @pl.loop(0, DEPTH)
        def _(o):
            hand(o).wait_send()

    if stop == 4:
        finish_x()
        finish_rs()
        finish_ag()
        out_ref[...] = gram[0:7].reshape(ROWS, BLOCK)[:, :COLS]
        return

    def t_part(q):
        return jnp.dot(
            gram[pl.ds(q * 7, 7)].reshape(ROWS, BLOCK), xi_all, preferred_element_type=jnp.float32
        )

    def t_copy(k):
        where = at((x + k) % SIDE, y, c)
        return remote(t_out.at[k], t_in.at[k], t_send.at[k], t_recv.at[k], where)

    for k in (2, 1, 3):
        t_out[k] = t_part((x + k) % SIDE).astype(jnp.bfloat16)
        t_copy(k).start()
    t_sum = t_part(x)
    gram_t[...] = gram[0 : 2 * USED].reshape(BLOCK, BLOCK).T.reshape(SIDE, ROWS, BLOCK)
    for k in (1, 3, 2):
        t_copy(k).wait_recv()
        t_sum += t_in[k].astype(jnp.float32)

    u[x] = (coef_quad * xj[x].astype(jnp.float32) + coef_cubic * t_sum).astype(jnp.bfloat16)

    def u_copy(k):
        where = at((x + k) % SIDE, y, c)
        return remote(u.at[x], u.at[x], u_send.at[k], u_recv.at[k], where)

    for k in (2, 1, 3):
        u_copy(k).start()
    for k in (1, 3, 2):
        arrived(u.at[(x + SIDE - k) % SIDE], u_recv.at[k])

    def finish_u():
        for k in (1, 2, 3):
            t_copy(k).wait_send()
            u_copy(k).wait_send()

    if stop == 5:
        finish_x()
        finish_rs()
        finish_ag()
        finish_u()
        out_ref[...] = u[0] + u[1] + u[2] + u[3] + gram_t[0, :, :COLS]
        return

    u_all = u[...].reshape(BLOCK, COLS)

    def p_copy(q):
        return remote(p_out.at[q], p_in.at[y], p_send.at[q], p_recv.at[y], from_i(q))

    for q in range(SIDE):
        local = jnp.logical_and(own_i, q == quarter)
        p_out[q] = jnp.dot(gram_t[q], u_all, preferred_element_type=jnp.float32).astype(
            jnp.bfloat16
        )

        @pl.when(local)
        def _():
            pltpu.make_async_copy(p_out.at[q], p_in.at[y], p_recv.at[y]).start()

        @pl.when(jnp.logical_not(local))
        def _():
            p_copy(q).start()

    finish_x()
    finish_rs()
    finish_ag()
    finish_u()
    result = coef_linear * m_ref[...].astype(jnp.float32)
    for k in range(SIDE):
        arrived(p_in.at[k], p_recv.at[k])
        result += p_in[k].astype(jnp.float32)
    out_ref[...] = (result * math.sqrt(max(M, N))).astype(jnp.bfloat16)
    for q in range(SIDE):

        @pl.when(jnp.logical_not(jnp.logical_and(own_i, q == quarter)))
        def _():
            p_copy(q).wait_send()


def body(momentum, stop=0):
    bf16, f32 = jnp.bfloat16, jnp.float32
    block = (SIDE, ROWS, COLS)
    ring = (8, CHUNK, BLOCK)
    sem = pltpu.SemaphoreType.DMA
    return pl.pallas_call(
        functools.partial(kernel, stop),
        out_shape=jax.ShapeDtypeStruct((ROWS, COLS), bf16),
        in_specs=[pl.BlockSpec(memory_space=pltpu.VMEM)],
        out_specs=pl.BlockSpec(memory_space=pltpu.VMEM),
        scratch_shapes=[
            pltpu.VMEM(block, bf16),
            pltpu.VMEM(block, bf16),
            pltpu.VMEM((DEPTH, CHUNK, BLOCK), f32),
            pltpu.VMEM((2, ROWS, BLOCK), bf16),
            pltpu.VMEM((2, ROWS, BLOCK), bf16),
            pltpu.VMEM(ring, bf16),
            pltpu.VMEM(ring, bf16),
            pltpu.VMEM(ring, bf16),
            pltpu.VMEM(ring, bf16),
            pltpu.VMEM((2 * DEPTH, CHUNK, BLOCK), bf16),
            pltpu.VMEM((SIDE, ROWS, BLOCK), bf16),
            pltpu.VMEM(block, bf16),
            pltpu.VMEM(block, bf16),
            pltpu.VMEM(block, bf16),
            pltpu.VMEM(block, bf16),
            pltpu.VMEM(block, bf16),
            sem((2, SIDE)), sem((2, SIDE)),
            sem((2,)), sem((2,)),
            sem((2, 8)), sem((2, 8)),
            sem((2, 8)), sem((2, 8)),
            sem((DEPTH,)), sem((DEPTH,)),
            sem((SIDE,)), sem((SIDE,)),
            sem((SIDE,)), sem((SIDE,)),
            sem((SIDE,)), sem((SIDE,)),
        ],
        compiler_params=pltpu.CompilerParams(
            collective_id=0, has_side_effects=True, vmem_limit_bytes=48 * 2**20
        ),
        cost_estimate=pl.CostEstimate(
            flops=6 * BLOCK * BLOCK * COLS, bytes_accessed=4 * ROWS * COLS, transcendentals=0
        ),
        name="newton_schulz",
    )(momentum)


def solution(mesh):
    return jax.shard_map(
        body,
        mesh=mesh,
        in_specs=(P("row", "col"),),
        out_specs=P("row", "col"),
        check_vma=False,
    )
```

time: 1050 us -> 150 us (0.14)
  waiting for transfers between devices: 985 us -> 0 us
  Pallas kernels: 0 us -> 148 us
  blocking collectives: 32 us -> 0 us
  between operations: 13.1 us -> 0.01 us
  matrix products: 13 us -> 0 us
    unnamed x5 -> x0, waiting for transfers between devices: 671 us -> none
    all_gather x3 -> x0, waiting for transfers between devices: 313 us -> none  [the longest x1 143 us: body(): lax.all_gather(poly, 'col', axis=1, tiled=True)]
    pallas_call x0 -> x1, Pallas kernels: none -> 148 us  [body(): pl.pallas_call(functools.partial(kernel, stop), out_shape=jax.ShapeDtypeS...]
    all_gather x1 -> x0, blocking collectives: 32 us -> none  [body(): lax.all_gather(own, 'row', axis=0, tiled=True)]
  transfers between devices with their start and end apart: 4 -> 0, of which waited for: 4 -> 0; matrix products, arithmetic and copies ran while one was open for 0% -> 0% of each run, Pallas kernels for 0% -> 0%
where the time goes in v1:
time: 150 us
  Pallas kernels  148 us (99%)
  local copies, waits for them, and re-layouts  1.67 us (1%)
    pallas_call x1, Pallas kernels, body(): pl.pallas_call(functools.partial(kernel, stop), out_shape=jax.ShapeDtypeS...  148 us

profile of v1, /device:TPU:1, one launch (start us, length us, event | category | flops | bytes accessed | tf_op | source)
XLA Modules:
  0.0 149.5 jit_solution(11719034660748184580)
XLA Ops:
  0.0 0.0 copy-start
  0.0 1.0 copy-done
  1.0 147.8 %newton_schulz.1 = bf16[224,576]{1,0:T(8,128)(2,1)S(1)} custom-call(bf16[224,576]{1,0:T(8,128)(2,1)S(1)} %copy-done), custom_call_target="tpu_custom_call" | custom-call | flops 2774532096 | bytes 516096 | tf_op jit(solution)/shard_map/newton_schulz/pallas_call | solution.py:362
  148.8 0.7 copy.3
Async XLA Ops:
  0.0 1.0 copy-start

commit v2 on v0

v2 whole, which is shorter than its diff:
```python
import functools
import math

import jax
import jax.numpy as jnp
from jax import lax
from jax.experimental import pallas as pl
from jax.experimental.pallas import tpu as pltpu
from jax.sharding import PartitionSpec as P

M = 3584
N = 18432

coef_linear = 3.4445
coef_quad = -4.775
coef_cubic = 2.0315

SIDE = 4
DEPTH = 16
BLOCK = M // SIDE
ROWS = BLOCK // SIDE
COLS = N // 32
PART = ROWS // 2
PIECE = 32
PADDED = 4 * PIECE
GROUPS = ((0, 256), (256, COLS - 256))
NT = (((1,), (1,)), ((), ()))


def kernel(
    stop, m_ref, out_ref, xi, xj, acc, sib_out, sib_in, near_out, near_in, cls, far_out, far_in,
    gram, gram_t, t_out, t_in, t_sum, u, p_out, p_in,
    i_send, i_recv, j_send, j_recv, s_send, s_recv, near_send, near_recv, far_send, far_recv,
    gf_send, gf_recv, gn_send, gn_recv, h_send, h_recv,
    t_send, t_recv, u_send, u_recv, p_send, p_recv,
):
    row, col = lax.axis_index("row"), lax.axis_index("col")
    x, y_lo, c = row // 4, (row // 2) % 2, row % 2
    z, y_hi = col // 2, col % 2
    y = y_hi * 2 + y_lo
    quarter = y_lo * 2 + c
    r, a = z % 4, z // 4
    bf16, f32 = jnp.bfloat16, jnp.float32

    def at(x_, y_, c_):
        return ((x_ * 2 + y_ % 2) * 2 + c_, z * 2 + y_ // 2)

    def along(d):
        return (row, ((z + d + DEPTH) % DEPTH) * 2 + y_hi)

    def remote(src, dst, send, recv, where):
        return pltpu.make_async_remote_copy(
            src_ref=src, dst_ref=dst, send_sem=send, recv_sem=recv,
            device_id=where, device_id_type=pl.DeviceIdType.MESH,
        )

    def arrived(dst, recv):
        pltpu.make_async_copy(dst, dst, recv).wait()

    def to_i(k):
        return at(x, k, y_hi)

    def from_i(k):
        return at(x, c * 2 + k // 2, k % 2)

    sibling = at(x, y, 1 - c)
    partner = at(x, c * 2 + y_lo, y_hi)
    own = c == y_hi
    others = jnp.logical_not(own)
    near = (1, -1, 2 - 4 * c)

    barrier = pltpu.get_barrier_semaphore()

    def signal(where):
        pl.semaphore_signal(barrier, inc=1, device_id=where, device_id_type=pl.DeviceIdType.MESH)

    signal(sibling)
    for d in (1, -1, 2, -2, 4, -4, 8):
        signal(along(d))
    for k in (1, 2, 3):
        signal(at((x + k) % SIDE, y, c))
    for k in range(SIDE):

        @pl.when(jnp.logical_not(jnp.logical_and(own, y == k)))
        def _():
            signal(to_i(k))

        @pl.when(jnp.logical_not(jnp.logical_and(own, quarter == k)))
        def _():
            signal(from_i(k))

    @pl.when(others)
    def _():
        signal(partner)

    pl.semaphore_wait(barrier, 20 - 3 * own.astype(jnp.int32))

    def j_first():
        return remote(m_ref, xj.at[x], j_send.at[0], j_recv.at[0], partner)

    def i_copy(k):
        return remote(
            m_ref, xi.at[quarter], i_send.at[k], i_recv.at[quarter], to_i((y + k) % SIDE)
        )

    def j_copy(k):
        where = at((x + k) % SIDE, y, c)
        return remote(xj.at[x], xj.at[x], j_send.at[k], j_recv.at[k], where)

    @pl.when(own)
    def _():
        pltpu.make_async_copy(m_ref, xj.at[x], j_recv.at[0]).start()
        pltpu.make_async_copy(m_ref, xi.at[quarter], i_recv.at[quarter]).start()

    @pl.when(others)
    def _():
        j_first().start()
        i_copy(0).start()

    for k in (2, 1, 3):
        i_copy(k).start()
    arrived(xj.at[x], j_recv.at[0])
    for k in (2, 1, 3):
        j_copy(k).start()
    for k in range(SIDE):
        arrived(xi.at[k], i_recv.at[k])
    for k in (1, 2, 3):
        arrived(xj.at[(x + SIDE - k) % SIDE], j_recv.at[k])

    def finish():
        @pl.when(others)
        def _():
            j_first().wait_send()
            i_copy(0).wait_send()

        for k in (1, 2, 3):
            i_copy(k).wait_send()
            j_copy(k).wait_send()
        if stop == 1:
            return
        for k in range(2):
            s_copy(k).wait_send()
        if stop == 2:
            return
        for k in range(3):
            near_copy(k).wait_send()
            far_copy(k).wait_send()
        if stop == 3:
            return
        for k in range(3):
            gf_copy(k).wait_send()
            gn_copy(k).wait_send()
        for k in range(4):
            hand(k).wait_send()
        if stop == 4:
            return
        for g in range(2):
            for k in (1, 2, 3):
                t_copy(g, k).wait_send()
                u_copy(g, k).wait_send()

    if stop == 1:
        finish()
        out_ref[...] = xi[0] + xj[0]
        return

    def s_copy(k):
        part = pl.ds(2 * k, 2)
        return remote(sib_out.at[part], sib_in.at[part], s_send.at[k], s_recv.at[k], sibling)

    xi_all = xi[...].reshape(BLOCK, COLS)
    for k in range(2):
        term = lax.dot_general(xj[(1 - c) * 2 + k], xi_all, NT, preferred_element_type=f32)
        sib_out[2 * k : 2 * k + 2] = term.astype(bf16).reshape(2, PART, BLOCK)
        s_copy(k).start()
    for k in range(2):
        term = lax.dot_general(xj[c * 2 + k], xi_all, NT, preferred_element_type=f32)
        acc[2 * k : 2 * k + 2] = term.reshape(2, PART, BLOCK)
    for k in range(2):
        s_copy(k).wait_recv()

    if stop == 2:
        finish()
        out_ref[0:PART] = (acc[0] + sib_in[0].astype(f32))[:, :COLS].astype(bf16)
        return

    def near_copy(k):
        return remote(
            near_out.at[k], near_in.at[k], near_send.at[k], near_recv.at[k], along(near[k])
        )

    for k in (2, 0, 1):
        q = (r + near[k] + 4) % 4
        near_out[k] = (acc[q] + sib_in[q].astype(f32)).astype(bf16)
        near_copy(k).start()
    cls[0:PART] = acc[r] + sib_in[r].astype(f32)
    cls[PART:] = jnp.zeros_like(cls[PART:])
    for k in (0, 1, 2):
        near_copy(k).wait_recv()
        cls[0:PART] += near_in[k].astype(f32)
    far_out[...] = cls[...].astype(bf16)

    def far_copy(k):
        piece = pl.ds(((a + k + 1) % 4) * PIECE, PIECE)
        where = along(4 * (k + 1))
        return remote(far_out.at[piece], far_in.at[k], far_send.at[k], far_recv.at[k], where)

    for k in (1, 0, 2):
        far_copy(k).start()
    total = cls[pl.ds(a * PIECE, PIECE)]
    for k in (0, 2, 1):
        far_copy(k).wait_recv()
        total += far_in[k].astype(f32)
    gram[c, r, pl.ds(a * PIECE, PIECE)] = total.astype(bf16)

    if stop == 3:
        finish()
        out_ref[0:PIECE] = gram[c, r, pl.ds(a * PIECE, PIECE)][:, :COLS]
        return

    def gf_copy(k):
        piece = gram.at[c, r, pl.ds(a * PIECE, PIECE)]
        return remote(piece, piece, gf_send.at[k], gf_recv.at[k], along(4 * (k + 1)))

    def gn_copy(k):
        part = gram.at[c, r, pl.ds(0, PART)]
        return remote(part, part, gn_send.at[k], gn_recv.at[k], along(near[k]))

    def hand(k):
        part = gram.at[c, (r + k) % 4, pl.ds(0, PART)]
        return remote(part, part, h_send.at[k], h_recv.at[k], sibling)

    for k in (1, 0, 2):
        gf_copy(k).start()
    for k in (0, 2, 1):
        arrived(gram.at[c, r, pl.ds(((a + 3 - k) % 4) * PIECE, PIECE)], gf_recv.at[k])
    for k in (2, 0, 1):
        gn_copy(k).start()
    hand(0).start()
    for k in (0, 1, 2):
        arrived(gram.at[c, (r - near[k] + 4) % 4, pl.ds(0, PART)], gn_recv.at[k])
        hand((3, 1, 2)[k]).start()
    for k in range(4):
        arrived(gram.at[1 - c, (r + k) % 4, pl.ds(0, PART)], h_recv.at[k])

    if stop == 4:
        finish()
        out_ref[0:PART] = gram[0, 0, 0:PART, :COLS]
        return

    def columns(g):
        return pl.ds(*GROUPS[g])

    def t_part(g, q):
        rows = gram[q // 2, pl.ds((q % 2) * 2, 2), 0:PART].reshape(ROWS, BLOCK)
        right = xi[:, :, columns(g)].reshape(BLOCK, GROUPS[g][1])
        return jnp.dot(rows, right, preferred_element_type=f32)

    def t_copy(g, k):
        where = at((x + k) % SIDE, y, c)
        part = columns(g)
        return remote(
            t_out.at[k, :, part], t_in.at[k, :, part], t_send.at[g, k], t_recv.at[g, k], where
        )

    def u_copy(g, k):
        where = at((x + k) % SIDE, y, c)
        part = u.at[x, :, columns(g)]
        return remote(part, part, u_send.at[g, k], u_recv.at[g, k], where)

    for g in range(2):
        for k in (2, 1, 3):
            t_out[k, :, columns(g)] = t_part(g, (x + k) % SIDE).astype(bf16)
            t_copy(g, k).start()
    for g in range(2):
        t_sum[:, columns(g)] = t_part(g, x)
    gram_t[...] = (
        gram[:, :, 0:PART].reshape(BLOCK, BLOCK).T.reshape(SIDE, ROWS, BLOCK)
    )
    for g in range(2):
        part = columns(g)
        for k in (1, 3, 2):
            t_copy(g, k).wait_recv()
            t_sum[:, part] += t_in[k, :, part].astype(f32)
        u[x, :, part] = (
            coef_quad * xj[x, :, part].astype(f32) + coef_cubic * t_sum[:, part]
        ).astype(bf16)
        for k in (2, 1, 3):
            u_copy(g, k).start()

    def p_copy(g, q):
        part = columns(g)
        return remote(
            p_out.at[q, :, part], p_in.at[y, :, part], p_send.at[g, q], p_recv.at[g, y], from_i(q)
        )

    for g in range(2):
        part = columns(g)
        for k in (1, 3, 2):
            arrived(u.at[(x + SIDE - k) % SIDE, :, part], u_recv.at[g, k])
        right = u[:, :, part].reshape(BLOCK, GROUPS[g][1])
        for q in range(SIDE):
            local = jnp.logical_and(own, q == quarter)
            p_out[q, :, part] = jnp.dot(gram_t[q], right, preferred_element_type=f32).astype(bf16)

            @pl.when(local)
            def _():
                pltpu.make_async_copy(
                    p_out.at[q, :, part], p_in.at[y, :, part], p_recv.at[g, y]
                ).start()

            @pl.when(jnp.logical_not(local))
            def _():
                p_copy(g, q).start()

    finish()
    for g in range(2):
        part = columns(g)
        result = coef_linear * m_ref[:, part].astype(f32)
        for k in range(SIDE):
            arrived(p_in.at[k, :, part], p_recv.at[g, k])
            result += p_in[k, :, part].astype(f32)
        out_ref[:, part] = (result * math.sqrt(max(M, N))).astype(bf16)
    for g in range(2):
        for q in range(SIDE):

            @pl.when(jnp.logical_not(jnp.logical_and(own, q == quarter)))
            def _():
                p_copy(g, q).wait_send()


def body(momentum, stop=0):
    bf16, f32 = jnp.bfloat16, jnp.float32
    block = (SIDE, ROWS, COLS)
    sem = pltpu.SemaphoreType.DMA
    return pl.pallas_call(
        functools.partial(kernel, stop),
        out_shape=jax.ShapeDtypeStruct((ROWS, COLS), bf16),
        in_specs=[pl.BlockSpec(memory_space=pltpu.VMEM)],
        out_specs=pl.BlockSpec(memory_space=pltpu.VMEM),
        scratch_shapes=[
            pltpu.VMEM(block, bf16),
            pltpu.VMEM(block, bf16),
            pltpu.VMEM((4, PART, BLOCK), f32),
            pltpu.VMEM((4, PART, BLOCK), bf16),
            pltpu.VMEM((4, PART, BLOCK), bf16),
            pltpu.VMEM((3, PART, BLOCK), bf16),
            pltpu.VMEM((3, PART, BLOCK), bf16),
            pltpu.VMEM((PADDED, BLOCK), f32),
            pltpu.VMEM((PADDED, BLOCK), bf16),
            pltpu.VMEM((3, PIECE, BLOCK), bf16),
            pltpu.VMEM((2, 4, PADDED, BLOCK), bf16),
            pltpu.VMEM((SIDE, ROWS, BLOCK), bf16),
            pltpu.VMEM(block, bf16),
            pltpu.VMEM(block, bf16),
            pltpu.VMEM((ROWS, COLS), f32),
            pltpu.VMEM(block, bf16),
            pltpu.VMEM(block, bf16),
            pltpu.VMEM(block, bf16),
            sem((SIDE,)), sem((SIDE,)),
            sem((SIDE,)), sem((SIDE,)),
            sem((2,)), sem((2,)),
            sem((3,)), sem((3,)),
            sem((3,)), sem((3,)),
            sem((3,)), sem((3,)),
            sem((3,)), sem((3,)),
            sem((4,)), sem((4,)),
            sem((2, SIDE)), sem((2, SIDE)),
            sem((2, SIDE)), sem((2, SIDE)),
            sem((2, SIDE)), sem((2, SIDE)),
        ],
        compiler_params=pltpu.CompilerParams(
            collective_id=0, has_side_effects=True, vmem_limit_bytes=48 * 2**20
        ),
        cost_estimate=pl.CostEstimate(
            flops=6 * BLOCK * BLOCK * COLS, bytes_accessed=4 * ROWS * COLS, transcendentals=0
        ),
        name="newton_schulz",
    )(momentum)


def solution(mesh):
    return jax.shard_map(
        body,
        mesh=mesh,
        in_specs=(P("row", "col"),),
        out_specs=P("row", "col"),
        check_vma=False,
    )
```

time: 1050 us -> 125 us (0.12)
  waiting for transfers between devices: 985 us -> 0 us
  Pallas kernels: 0 us -> 123 us
  blocking collectives: 32 us -> 0 us
  between operations: 13.1 us -> 0.01 us
  matrix products: 13 us -> 0 us
    unnamed x5 -> x0, waiting for transfers between devices: 671 us -> none
    all_gather x3 -> x0, waiting for transfers between devices: 313 us -> none  [the longest x1 143 us: body(): lax.all_gather(poly, 'col', axis=1, tiled=True)]
    pallas_call x0 -> x1, Pallas kernels: none -> 123 us  [body(): pl.pallas_call(functools.partial(kernel, stop), out_shape=jax.ShapeDtypeS...]
    all_gather x1 -> x0, blocking collectives: 32 us -> none  [body(): lax.all_gather(own, 'row', axis=0, tiled=True)]
  transfers between devices with their start and end apart: 4 -> 0, of which waited for: 4 -> 0; matrix products, arithmetic and copies ran while one was open for 0% -> 0% of each run, Pallas kernels for 0% -> 0%
where the time goes in v2:
time: 125 us
  Pallas kernels  123 us (98%)
  local copies, waits for them, and re-layouts  1.67 us (1%)
    pallas_call x1, Pallas kernels, body(): pl.pallas_call(functools.partial(kernel, stop), out_shape=jax.ShapeDtypeS...  123 us

profile of v2, /device:TPU:1, one launch (start us, length us, event | category | flops | bytes accessed | tf_op | source)
XLA Modules:
  0.0 124.8 jit_solution(7291960446403278517)
XLA Ops:
  0.0 0.0 copy-start
  0.0 1.0 copy-done
  1.0 123.2 %newton_schulz.1 = bf16[224,576]{1,0:T(8,128)(2,1)S(1)} custom-call(bf16[224,576]{1,0:T(8,128)(2,1)S(1)} %copy-done), custom_call_target="tpu_custom_call" | custom-call | flops 2774532096 | bytes 516096 | tf_op jit(solution)/shard_map/newton_schulz/pallas_call | solution.py:336
  124.1 0.7 copy.3
Async XLA Ops:
  0.0 1.0 copy-start

commit v3 on v0

v3 whole, which is shorter than its diff:
```python
import math

import jax
import jax.numpy as jnp
from jax import lax
from jax.experimental import pallas as pl
from jax.experimental.pallas import tpu as pltpu
from jax.sharding import PartitionSpec as P

M = 3584
N = 18432

coef_linear = 3.4445
coef_quad = -4.775
coef_cubic = 2.0315

SIDE = 4
DEPTH = 16
BLOCK = M // SIDE
ROWS = BLOCK // SIDE
COLS = N // 32
PART = ROWS // 2
PIECE = 32
PADDED = 4 * PIECE
HALVES = ((0, 512), (512, BLOCK - 512))
SHARES = ((0, 128), (128, ROWS - 128))
FIRST = pl.ds(0, 256)
SECOND = pl.ds(256, COLS - 256)
NT = (((1,), (1,)), ((), ()))


def kernel(
    m_ref, out_ref, swap, xi, xj, acc, sib_out, sib_in, near_out, near_in, cls, far_out, far_in,
    gram, gram_t, tx_out, tx_in, tx_sum, ty_out, ty_in, ux, uy, px_out, px_in, py_out, py_in,
    fin_out, fin_in,
    i_send, i_recv, j_send, j_recv, s_send, s_recv, near_send, near_recv, far_send, far_recv,
    gf_send, gf_recv, gn_send, gn_recv, h_send, h_recv, w_send, w_recv,
    tx_send, tx_recv, ty_send, ty_recv, ux_send, ux_recv, uy_send, uy_recv,
    px_send, px_recv, py_send, py_recv, fin_send, fin_recv,
):
    row, col = lax.axis_index("row"), lax.axis_index("col")
    x, y_lo, c = row // 4, (row // 2) % 2, row % 2
    z, y_hi = col // 2, col % 2
    y = y_hi * 2 + y_lo
    quarter = y_lo * 2 + c
    r, a = z % 4, z // 4
    bf16, f32 = jnp.bfloat16, jnp.float32

    def at(x_, y_, c_):
        return ((x_ * 2 + y_ % 2) * 2 + c_, z * 2 + y_ // 2)

    def along(d):
        return (row, ((z + d + DEPTH) % DEPTH) * 2 + y_hi)

    def remote(src, dst, send, recv, where):
        return pltpu.make_async_remote_copy(
            src_ref=src, dst_ref=dst, send_sem=send, recv_sem=recv,
            device_id=where, device_id_type=pl.DeviceIdType.MESH,
        )

    def arrived(dst, recv):
        pltpu.make_async_copy(dst, dst, recv).wait()

    def to_i(k):
        return at(x, k, y_hi)

    def from_i(k):
        return at(x, c * 2 + k // 2, k % 2)

    def on_x(k):
        return at((x + k) % SIDE, y, c)

    def on_y(k):
        return at(x, (y + k) % SIDE, c)

    sibling = at(x, y, 1 - c)
    peer = at(x, (y + 2) % SIDE, 1 - c)
    own = c == y_hi
    others = jnp.logical_not(own)
    near = (1, -1, 2 - 4 * c)

    barrier = pltpu.get_barrier_semaphore()

    def signal(where):
        pl.semaphore_signal(barrier, inc=1, device_id=where, device_id_type=pl.DeviceIdType.MESH)

    for d in (8, 4, -4, 2, -2, 1, -1):
        signal(along(d))
    for k in (2, 1, 3):
        signal(on_x(k))
        signal(on_y(k))
    for k in range(SIDE):

        @pl.when(jnp.logical_not(jnp.logical_and(own, y == k)))
        def _():
            signal(to_i(k))

        @pl.when(jnp.logical_not(jnp.logical_and(own, quarter == k)))
        def _():
            signal(from_i(k))

    signal(peer)
    signal(sibling)
    pl.semaphore_wait(barrier, 23 - 2 * own.astype(jnp.int32))

    def block(ref, k):
        return ref.at[pl.ds(pl.multiple_of(k * ROWS, ROWS), ROWS)]

    common = y_lo * 2 + y_hi
    handed = y_lo * 2 + 1 - y_hi
    swap_copy = remote(m_ref, swap, w_send.at[0], w_recv.at[0], peer)

    def hand_i(src):
        return remote(src, block(xi, handed), i_send.at[0], i_recv.at[handed], sibling)

    def i_copy(k):
        there = block(xi, quarter)
        return remote(m_ref, there, i_send.at[k], i_recv.at[quarter], to_i((y + k) % SIDE))

    def j_copy(src, k):
        return remote(src, block(xj, x), j_send.at[k], j_recv.at[k], on_x(k))

    def keep(src):
        common_rows = pl.ds(pl.multiple_of(common * ROWS, ROWS), ROWS)
        xi[common_rows] = src[...]
        x_rows = pl.ds(pl.multiple_of(x * ROWS, ROWS), ROWS)
        xj[x_rows] = src[...]

    swap_copy.start()

    @pl.when(own)
    def _():
        for k in (2, 1, 3):
            j_copy(m_ref, k).start()
        keep(m_ref)

    @pl.when(others)
    def _():
        hand_i(m_ref).start()

    swap_copy.wait_recv()

    @pl.when(own)
    def _():
        hand_i(swap).start()

    @pl.when(others)
    def _():
        for k in (2, 1, 3):
            j_copy(swap, k).start()

    for k in (1, 3):
        i_copy(k).start()

    @pl.when(others)
    def _():
        keep(swap)

    arrived(block(xi, handed), i_recv.at[handed])
    for k in range(2):
        far_slot = (1 - y_lo) * 2 + k
        arrived(block(xi, far_slot), i_recv.at[far_slot])
    for k in (1, 2, 3):
        arrived(block(xj, (x + SIDE - k) % SIDE), j_recv.at[k])

    def half(g):
        return pl.ds(*HALVES[g])

    def s_copy(g):
        return remote(
            sib_out.at[:, :, half(g)], sib_in.at[:, :, half(g)], s_send.at[g], s_recv.at[g], sibling
        )

    def terms(core, g):
        rows = pl.ds(pl.multiple_of(core * (BLOCK // 2), BLOCK // 2), BLOCK // 2)
        return lax.dot_general(xi[rows], xj[half(g)], NT, preferred_element_type=f32).reshape(
            4, PART, HALVES[g][1]
        )

    for g in range(2):
        sib_out[:, :, half(g)] = terms(1 - c, g).astype(bf16)
        s_copy(g).start()
        acc[:, :, half(g)] = terms(c, g)

    def near_copy(g, k):
        return remote(
            near_out.at[k, :, half(g)], near_in.at[k, :, half(g)],
            near_send.at[g, k], near_recv.at[g, k], along(near[k]),
        )

    def far_copy(g, k):
        piece = pl.ds(pl.multiple_of(((a + k + 1) % 4) * PIECE, PIECE), PIECE)
        return remote(
            far_out.at[piece, half(g)], far_in.at[k, :, half(g)],
            far_send.at[g, k], far_recv.at[g, k], along(4 * (k + 1)),
        )

    def mine(k=0):
        return pl.ds(pl.multiple_of(((a + 4 - k) % 4) * PIECE, PIECE), PIECE)

    def gf_copy(g, k):
        piece = gram.at[c, r, mine(), half(g)]
        return remote(piece, piece, gf_send.at[g, k], gf_recv.at[g, k], along(4 * (k + 1)))

    def quarter_of(core, q, g):
        return gram.at[core, q, pl.ds(0, PART), half(g)]

    def gn_copy(g, k):
        part = quarter_of(c, r, g)
        return remote(part, part, gn_send.at[g, k], gn_recv.at[g, k], along(near[k]))

    def hand(g, k):
        part = quarter_of(c, (r + k) % 4, g)
        return remote(part, part, h_send.at[g, k], h_recv.at[g, k], sibling)

    cls[PART:] = jnp.zeros_like(cls[PART:])
    for g in range(2):
        s_copy(g).wait_recv()
        for k in (2, 0, 1):
            q = (r + near[k] + 4) % 4
            near_out[k, :, half(g)] = (
                acc[q, :, half(g)] + sib_in[q, :, half(g)].astype(f32)
            ).astype(bf16)
            near_copy(g, k).start()
        cls[0:PART, half(g)] = acc[r, :, half(g)] + sib_in[r, :, half(g)].astype(f32)
    for g in range(2):
        for k in (0, 1, 2):
            near_copy(g, k).wait_recv()
        cls[0:PART, half(g)] += (
            near_in[0, :, half(g)].astype(f32)
            + near_in[1, :, half(g)].astype(f32)
            + near_in[2, :, half(g)].astype(f32)
        )
        far_out[:, half(g)] = cls[:, half(g)].astype(bf16)
        for k in (1, 0, 2):
            far_copy(g, k).start()

    for g in range(2):
        total = cls[mine(), half(g)]
        for k in (0, 2, 1):
            far_copy(g, k).wait_recv()
            total += far_in[k, :, half(g)].astype(f32)
        gram[c, r, mine(), half(g)] = total.astype(bf16)
        for k in (1, 0, 2):
            gf_copy(g, k).start()
    for g in range(2):
        for k in (0, 2, 1):
            arrived(gram.at[c, r, mine(k + 1), half(g)], gf_recv.at[g, k])
        for k in (2, 0, 1):
            gn_copy(g, k).start()
        hand(g, 0).start()

    def share(g):
        return pl.ds(*SHARES[g])

    def rows_of(g, q):
        first, size = HALVES[g][0], SHARES[g][1]
        return pl.ds(pl.multiple_of(first + q * size, PIECE), size)

    def rows_at(q):
        return pl.ds(pl.multiple_of(q * ROWS, ROWS), ROWS)

    def gram_rows(q):
        return gram[q // 2, pl.ds((q % 2) * 2, 2), 0:PART].reshape(ROWS, BLOCK)

    def dot(left, right):
        return jnp.dot(left, right, preferred_element_type=f32)

    def tx_copy(g, k):
        return remote(
            tx_out.at[k, share(g)], tx_in.at[k, share(g)],
            tx_send.at[g, k], tx_recv.at[g, k], on_x(k),
        )

    def ty_copy(k):
        return remote(ty_out.at[k], ty_in.at[k], ty_send.at[k], ty_recv.at[k], on_y(k))

    for g in range(2):
        for k in (0, 1, 2):
            arrived(quarter_of(c, (r - near[k] + 4) % 4, g), gn_recv.at[g, k])
            hand(g, (3, 1, 2)[k]).start()
        for k in (0, 3, 1, 2):
            arrived(quarter_of(1 - c, (r + k) % 4, g), h_recv.at[g, k])
        if g == 1:
            for k in (2, 1, 3):
                ty_out[k] = dot(gram_rows((y + k) % SIDE), xj[:, FIRST]).astype(bf16)
                ty_copy(k).start()
        gram_t[half(g)] = gram[:, :, 0:PART, half(g)].reshape(BLOCK, HALVES[g][1]).T
        for k in (2, 1, 3):
            tx_out[k, share(g)] = dot(gram_t[rows_of(g, (x + k) % SIDE)], xi[:, SECOND]).astype(
                bf16
            )
            tx_copy(g, k).start()
        tx_sum[share(g)] = dot(gram_t[rows_of(g, x)], xi[:, SECOND])

    def ux_copy(g, k):
        here = ux.at[rows_of(g, x)]
        return remote(here, here, ux_send.at[g, k], ux_recv.at[g, k], on_x(k))

    def uy_copy(k):
        here = uy.at[rows_at(y)]
        return remote(here, here, uy_send.at[k], uy_recv.at[k], on_y(k))

    def ux_part(g):
        total = tx_sum[share(g)]
        for k in (1, 3, 2):
            tx_copy(g, k).wait_recv()
            total += tx_in[k, share(g)].astype(f32)
        ux[rows_of(g, x)] = (
            coef_quad * xj[rows_of(g, x), SECOND].astype(f32) + coef_cubic * total
        ).astype(bf16)
        for k in (2, 1, 3):
            ux_copy(g, k).start()

    ux_part(0)
    total = dot(gram_rows(y), xj[:, FIRST])
    for k in (1, 3, 2):
        ty_copy(k).wait_recv()
        total += ty_in[k].astype(f32)
    uy[rows_at(y)] = (
        coef_quad * xi[rows_at(y), FIRST].astype(f32) + coef_cubic * total
    ).astype(bf16)
    for k in (2, 1, 3):
        uy_copy(k).start()
    ux_part(1)

    def px_copy(k):
        return remote(px_out.at[k], px_in.at[k], px_send.at[k], px_recv.at[k], on_x(k))

    def py_copy(q):
        return remote(py_out.at[q], py_in.at[y], py_send.at[q], py_recv.at[y], from_i(q))

    for k in (1, 3, 2):
        arrived(uy.at[rows_at((y + SIDE - k) % SIDE)], uy_recv.at[k])
    for k in (2, 1, 3):
        px_out[k] = dot(gram_t[rows_at((x + k) % SIDE)], uy[...]).astype(bf16)
        px_copy(k).start()
    for g in range(2):
        for k in (1, 3, 2):
            arrived(ux.at[rows_of(g, (x + SIDE - k) % SIDE)], ux_recv.at[g, k])
    for q in range(SIDE):
        local = jnp.logical_and(own, q == quarter)
        py_out[q] = dot(gram_rows(q), ux[...]).astype(bf16)

        @pl.when(local)
        def _():
            pltpu.make_async_copy(py_out.at[q], py_in.at[y], py_recv.at[y]).start()

        @pl.when(jnp.logical_not(local))
        def _():
            py_copy(q).start()

    factor = math.sqrt(max(M, N))
    total = dot(gram_t[rows_at(x)], uy[...])
    total += coef_linear * xj[rows_at(x), FIRST].astype(f32)
    for k in (1, 3, 2):
        px_copy(k).wait_recv()
        total += px_in[k].astype(f32)
    fin_out[...] = (total * factor).astype(bf16)
    fin_copy = remote(fin_out, fin_in, fin_send.at[0], fin_recv.at[0], peer)

    @pl.when(own)
    def _():
        out_ref[:, FIRST] = fin_out[...]

    @pl.when(others)
    def _():
        fin_copy.start()

    swap_copy.wait_send()
    hand_i(m_ref).wait_send()
    for k in (1, 3):
        i_copy(k).wait_send()
    for k in (1, 2, 3):
        j_copy(m_ref, k).wait_send()
    for g in range(2):
        s_copy(g).wait_send()
        for k in range(3):
            near_copy(g, k).wait_send()
            far_copy(g, k).wait_send()
            gf_copy(g, k).wait_send()
            gn_copy(g, k).wait_send()
        for k in range(4):
            hand(g, k).wait_send()
        for k in (1, 2, 3):
            tx_copy(g, k).wait_send()
            ux_copy(g, k).wait_send()
    for k in (1, 2, 3):
        ty_copy(k).wait_send()
        uy_copy(k).wait_send()
        px_copy(k).wait_send()

    result = coef_linear * m_ref[:, SECOND].astype(f32)
    for k in range(SIDE):
        arrived(py_in.at[k], py_recv.at[k])
        result += py_in[k].astype(f32)
    out_ref[:, SECOND] = (result * factor).astype(bf16)

    @pl.when(others)
    def _():
        fin_copy.wait_recv()
        out_ref[:, FIRST] = fin_in[...]
        fin_copy.wait_send()

    for q in range(SIDE):

        @pl.when(jnp.logical_not(jnp.logical_and(own, q == quarter)))
        def _():
            py_copy(q).wait_send()


def body(momentum):
    bf16, f32 = jnp.bfloat16, jnp.float32
    first = (SIDE, ROWS, FIRST.size)
    second = (SIDE, ROWS, SECOND.size)
    sem = pltpu.SemaphoreType.DMA
    return pl.pallas_call(
        kernel,
        out_shape=jax.ShapeDtypeStruct((ROWS, COLS), bf16),
        in_specs=[pl.BlockSpec(memory_space=pltpu.VMEM)],
        out_specs=pl.BlockSpec(memory_space=pltpu.VMEM),
        scratch_shapes=[
            pltpu.VMEM((ROWS, COLS), bf16),
            pltpu.VMEM((BLOCK, COLS), bf16),
            pltpu.VMEM((BLOCK, COLS), bf16),
            pltpu.VMEM((4, PART, BLOCK), f32),
            pltpu.VMEM((4, PART, BLOCK), bf16),
            pltpu.VMEM((4, PART, BLOCK), bf16),
            pltpu.VMEM((3, PART, BLOCK), bf16),
            pltpu.VMEM((3, PART, BLOCK), bf16),
            pltpu.VMEM((PADDED, BLOCK), f32),
            pltpu.VMEM((PADDED, BLOCK), bf16),
            pltpu.VMEM((3, PIECE, BLOCK), bf16),
            pltpu.VMEM((2, 4, PADDED, BLOCK), bf16),
            pltpu.VMEM((BLOCK, BLOCK), bf16),
            pltpu.VMEM(second, bf16),
            pltpu.VMEM(second, bf16),
            pltpu.VMEM(second[1:], f32),
            pltpu.VMEM(first, bf16),
            pltpu.VMEM(first, bf16),
            pltpu.VMEM((BLOCK, SECOND.size), bf16),
            pltpu.VMEM((BLOCK, FIRST.size), bf16),
            pltpu.VMEM(first, bf16),
            pltpu.VMEM(first, bf16),
            pltpu.VMEM(second, bf16),
            pltpu.VMEM(second, bf16),
            pltpu.VMEM(first[1:], bf16),
            pltpu.VMEM(first[1:], bf16),
            sem((SIDE,)), sem((SIDE,)),
            sem((SIDE,)), sem((SIDE,)),
            sem((2,)), sem((2,)),
            sem((2, 3)), sem((2, 3)),
            sem((2, 3)), sem((2, 3)),
            sem((2, 3)), sem((2, 3)),
            sem((2, 3)), sem((2, 3)),
            sem((2, 4)), sem((2, 4)),
            sem((1,)), sem((1,)),
            sem((2, SIDE)), sem((2, SIDE)),
            sem((SIDE,)), sem((SIDE,)),
            sem((2, SIDE)), sem((2, SIDE)),
            sem((SIDE,)), sem((SIDE,)),
            sem((SIDE,)), sem((SIDE,)),
            sem((SIDE,)), sem((SIDE,)),
            sem((1,)), sem((1,)),
        ],
        compiler_params=pltpu.CompilerParams(
            collective_id=0, has_side_effects=True, vmem_limit_bytes=48 * 2**20
        ),
        cost_estimate=pl.CostEstimate(
            flops=6 * BLOCK * BLOCK * COLS, bytes_accessed=4 * ROWS * COLS, transcendentals=0
        ),
        name="newton_schulz",
    )(momentum)


def solution(mesh):
    return jax.shard_map(
        body,
        mesh=mesh,
        in_specs=(P("row", "col"),),
        out_specs=P("row", "col"),
        check_vma=False,
    )
```

time: 1050 us -> 110 us (0.10)
  waiting for transfers between devices: 985 us -> 0 us
  Pallas kernels: 0 us -> 109 us
  blocking collectives: 32 us -> 0 us
  between operations: 13.1 us -> 0.01 us
  matrix products: 13 us -> 0 us
    unnamed x5 -> x0, waiting for transfers between devices: 671 us -> none
    all_gather x3 -> x0, waiting for transfers between devices: 313 us -> none  [the longest x1 143 us: body(): lax.all_gather(poly, 'col', axis=1, tiled=True)]
    pallas_call x0 -> x1, Pallas kernels: none -> 109 us  [body(): pl.pallas_call(kernel, out_shape=jax.ShapeDtypeStruct((ROWS, COLS), bf16)...]
    all_gather x1 -> x0, blocking collectives: 32 us -> none  [body(): lax.all_gather(own, 'row', axis=0, tiled=True)]
  transfers between devices with their start and end apart: 4 -> 0, of which waited for: 4 -> 0; matrix products, arithmetic and copies ran while one was open for 0% -> 0% of each run, Pallas kernels for 0% -> 0%
where the time goes in v3:
time: 110 us
  Pallas kernels  109 us (99%)
  local copies, waits for them, and re-layouts  1.67 us (2%)
    pallas_call x1, Pallas kernels, body(): pl.pallas_call(kernel, out_shape=jax.ShapeDtypeStruct((ROWS, COLS), bf16)...  109 us

profile of v3, /device:TPU:1, one launch (start us, length us, event | category | flops | bytes accessed | tf_op | source)
XLA Modules:
  0.0 110.2 jit_solution(9304575548429627231)
XLA Ops:
  0.0 0.0 copy-start
  0.0 1.0 copy-done
  1.0 108.6 %newton_schulz.1 = bf16[224,576]{1,0:T(8,128)(2,1)S(1)} custom-call(bf16[224,576]{1,0:T(8,128)(2,1)S(1)} %copy-done), custom_call_target="tpu_custom_call" | custom-call | flops 2774532096 | bytes 516096 | tf_op jit(solution)/shard_map/newton_schulz/pallas_call | solution.py:417
  109.5 0.7 copy.3
Async XLA Ops:
  0.0 1.0 copy-start

commit v4 on v3

--- a/solution.py
+++ b/solution.py
@@ -25,6 +25,7 @@
 HALVES = ((0, 512), (512, BLOCK - 512))
 SHARES = ((0, 128), (128, ROWS - 128))
 FIRST = pl.ds(0, 256)
+STRIP = 128
 SECOND = pl.ds(256, COLS - 256)
 NT = (((1,), (1,)), ((), ()))
 
@@ -36,7 +37,7 @@
     i_send, i_recv, j_send, j_recv, s_send, s_recv, near_send, near_recv, far_send, far_recv,
     gf_send, gf_recv, gn_send, gn_recv, h_send, h_recv, w_send, w_recv,
     tx_send, tx_recv, ty_send, ty_recv, ux_send, ux_recv, uy_send, uy_recv,
-    px_send, px_recv, py_send, py_recv, fin_send, fin_recv,
+    px_send, px_recv, py_send, py_recv, fin_send, fin_recv, inside,
 ):
     row, col = lax.axis_index("row"), lax.axis_index("col")
     x, y_lo, c = row // 4, (row // 2) % 2, row % 2
@@ -84,7 +85,7 @@
     def signal(where):
         pl.semaphore_signal(barrier, inc=1, device_id=where, device_id_type=pl.DeviceIdType.MESH)
 
-    for d in (8, 4, -4, 2, -2, 1, -1):
+    for d in (2, -2, 1, -1):
         signal(along(d))
     for k in (2, 1, 3):
         signal(on_x(k))
@@ -101,7 +102,15 @@
 
     signal(peer)
     signal(sibling)
-    pl.semaphore_wait(barrier, 23 - 2 * own.astype(jnp.int32))
+    pl.semaphore_wait(barrier, 20 - 2 * own.astype(jnp.int32))
+
+    def pass_on(k, d):
+        for e in (d, -d):
+            pl.semaphore_signal(
+                inside.at[k], inc=1, device_id=along(e), device_id_type=pl.DeviceIdType.MESH
+            )
+
+    pass_on(0, 2)
 
     def block(ref, k):
         return ref.at[pl.ds(pl.multiple_of(k * ROWS, ROWS), ROWS)]
@@ -162,6 +171,9 @@
         arrived(block(xi, far_slot), i_recv.at[far_slot])
     for k in (1, 2, 3):
         arrived(block(xj, (x + SIDE - k) % SIDE), j_recv.at[k])
+
+    pl.semaphore_wait(inside.at[0], 2)
+    pass_on(1, 4)
 
     def half(g):
         return pl.ds(*HALVES[g])
@@ -223,6 +235,7 @@
             ).astype(bf16)
             near_copy(g, k).start()
         cls[0:PART, half(g)] = acc[r, :, half(g)] + sib_in[r, :, half(g)].astype(f32)
+    pl.semaphore_wait(inside.at[1], 2)
     for g in range(2):
         for k in (0, 1, 2):
             near_copy(g, k).wait_recv()
@@ -272,8 +285,14 @@
             tx_send.at[g, k], tx_recv.at[g, k], on_x(k),
         )
 
-    def ty_copy(k):
-        return remote(ty_out.at[k], ty_in.at[k], ty_send.at[k], ty_recv.at[k], on_y(k))
+    def strip(f):
+        return pl.ds(f * STRIP, STRIP)
+
+    def ty_copy(f, k):
+        return remote(
+            ty_out.at[k, :, strip(f)], ty_in.at[k, :, strip(f)],
+            ty_send.at[f, k], ty_recv.at[f, k], on_y(k),
+        )
 
     for g in range(2):
         for k in (0, 1, 2):
@@ -282,9 +301,12 @@
         for k in (0, 3, 1, 2):
             arrived(quarter_of(1 - c, (r + k) % 4, g), h_recv.at[g, k])
         if g == 1:
-            for k in (2, 1, 3):
-                ty_out[k] = dot(gram_rows((y + k) % SIDE), xj[:, FIRST]).astype(bf16)
-                ty_copy(k).start()
+            for f in range(2):
+                for k in (2, 1, 3):
+                    ty_out[k, :, strip(f)] = dot(
+                        gram_rows((y + k) % SIDE), xj[:, strip(f)]
+                    ).astype(bf16)
+                    ty_copy(f, k).start()
         gram_t[half(g)] = gram[:, :, 0:PART, half(g)].reshape(BLOCK, HALVES[g][1]).T
         for k in (2, 1, 3):
             tx_out[k, share(g)] = dot(gram_t[rows_of(g, (x + k) % SIDE)], xi[:, SECOND]).astype(
@@ -297,9 +319,9 @@
         here = ux.at[rows_of(g, x)]
         return remote(here, here, ux_send.at[g, k], ux_recv.at[g, k], on_x(k))
 
-    def uy_copy(k):
-        here = uy.at[rows_at(y)]
-        return remote(here, here, uy_send.at[k], uy_recv.at[k], on_y(k))
+    def uy_copy(f, k):
+        here = uy.at[rows_at(y), strip(f)]
+        return remote(here, here, uy_send.at[f, k], uy_recv.at[f, k], on_y(k))
 
     def ux_part(g):
         total = tx_sum[share(g)]
@@ -313,28 +335,35 @@
             ux_copy(g, k).start()
 
     ux_part(0)
-    total = dot(gram_rows(y), xj[:, FIRST])
-    for k in (1, 3, 2):
-        ty_copy(k).wait_recv()
-        total += ty_in[k].astype(f32)
-    uy[rows_at(y)] = (
-        coef_quad * xi[rows_at(y), FIRST].astype(f32) + coef_cubic * total
-    ).astype(bf16)
-    for k in (2, 1, 3):
-        uy_copy(k).start()
+    for f in range(2):
+        total = dot(gram_rows(y), xj[:, strip(f)])
+        for k in (1, 3, 2):
+            ty_copy(f, k).wait_recv()
+            total += ty_in[k, :, strip(f)].astype(f32)
+        uy[rows_at(y), strip(f)] = (
+            coef_quad * xi[rows_at(y), strip(f)].astype(f32) + coef_cubic * total
+        ).astype(bf16)
+        for k in (2, 1, 3):
+            uy_copy(f, k).start()
     ux_part(1)
 
-    def px_copy(k):
-        return remote(px_out.at[k], px_in.at[k], px_send.at[k], px_recv.at[k], on_x(k))
+    def px_copy(f, k):
+        return remote(
+            px_out.at[k, :, strip(f)], px_in.at[k, :, strip(f)],
+            px_send.at[f, k], px_recv.at[f, k], on_x(k),
+        )
 
     def py_copy(q):
         return remote(py_out.at[q], py_in.at[y], py_send.at[q], py_recv.at[y], from_i(q))
 
-    for k in (1, 3, 2):
-        arrived(uy.at[rows_at((y + SIDE - k) % SIDE)], uy_recv.at[k])
-    for k in (2, 1, 3):
-        px_out[k] = dot(gram_t[rows_at((x + k) % SIDE)], uy[...]).astype(bf16)
-        px_copy(k).start()
+    for f in range(2):
+        for k in (1, 3, 2):
+            arrived(uy.at[rows_at((y + SIDE - k) % SIDE), strip(f)], uy_recv.at[f, k])
+        for k in (2, 1, 3):
+            px_out[k, :, strip(f)] = dot(
+                gram_t[rows_at((x + k) % SIDE)], uy[:, strip(f)]
+            ).astype(bf16)
+            px_copy(f, k).start()
     for g in range(2):
         for k in (1, 3, 2):
             arrived(ux.at[rows_of(g, (x + SIDE - k) % SIDE)], ux_recv.at[g, k])
@@ -351,21 +380,28 @@
             py_copy(q).start()
 
     factor = math.sqrt(max(M, N))
-    total = dot(gram_t[rows_at(x)], uy[...])
-    total += coef_linear * xj[rows_at(x), FIRST].astype(f32)
-    for k in (1, 3, 2):
-        px_copy(k).wait_recv()
-        total += px_in[k].astype(f32)
-    fin_out[...] = (total * factor).astype(bf16)
-    fin_copy = remote(fin_out, fin_in, fin_send.at[0], fin_recv.at[0], peer)
+
+    def fin_copy(f):
+        part = strip(f)
+        return remote(
+            fin_out.at[:, part], fin_in.at[:, part], fin_send.at[f], fin_recv.at[f], peer
+        )
+
+    for f in range(2):
+        total = dot(gram_t[rows_at(x)], uy[:, strip(f)])
+        total += coef_linear * xj[rows_at(x), strip(f)].astype(f32)
+        for k in (1, 3, 2):
+            px_copy(f, k).wait_recv()
+            total += px_in[k, :, strip(f)].astype(f32)
+        fin_out[:, strip(f)] = (total * factor).astype(bf16)
+
+        @pl.when(others)
+        def _():
+            fin_copy(f).start()
 
     @pl.when(own)
     def _():
         out_ref[:, FIRST] = fin_out[...]
-
-    @pl.when(others)
-    def _():
-        fin_copy.start()
 
     swap_copy.wait_send()
     hand_i(m_ref).wait_send()
@@ -385,10 +421,11 @@
         for k in (1, 2, 3):
             tx_copy(g, k).wait_send()
             ux_copy(g, k).wait_send()
-    for k in (1, 2, 3):
-        ty_copy(k).wait_send()
-        uy_copy(k).wait_send()
-        px_copy(k).wait_send()
+    for f in range(2):
+        for k in (1, 2, 3):
+            ty_copy(f, k).wait_send()
+            uy_copy(f, k).wait_send()
+            px_copy(f, k).wait_send()
 
     result = coef_linear * m_ref[:, SECOND].astype(f32)
     for k in range(SIDE):
@@ -398,9 +435,10 @@
 
     @pl.when(others)
     def _():
-        fin_copy.wait_recv()
-        out_ref[:, FIRST] = fin_in[...]
-        fin_copy.wait_send()
+        for f in range(2):
+            fin_copy(f).wait_recv()
+            out_ref[:, strip(f)] = fin_in[:, strip(f)]
+            fin_copy(f).wait_send()
 
     for q in range(SIDE):
 
@@ -456,12 +494,13 @@
             sem((2, 4)), sem((2, 4)),
             sem((1,)), sem((1,)),
             sem((2, SIDE)), sem((2, SIDE)),
-            sem((SIDE,)), sem((SIDE,)),
+            sem((2, SIDE)), sem((2, SIDE)),
+            sem((2, SIDE)), sem((2, SIDE)),
+            sem((2, SIDE)), sem((2, SIDE)),
             sem((2, SIDE)), sem((2, SIDE)),
             sem((SIDE,)), sem((SIDE,)),
-            sem((SIDE,)), sem((SIDE,)),
-            sem((SIDE,)), sem((SIDE,)),
-            sem((1,)), sem((1,)),
+            sem((2,)), sem((2,)),
+            pltpu.SemaphoreType.REGULAR((2,)),
         ],
         compiler_params=pltpu.CompilerParams(
             collective_id=0, has_side_effects=True, vmem_limit_bytes=48 * 2**20

time: 110 us -> 107 us (0.973)
  Pallas kernels: 109 us -> 106 us
    pallas_call x1, Pallas kernels: 109 us -> 106 us  [body(): pl.pallas_call(kernel, out_shape=jax.ShapeDtypeStruct((ROWS, COLS), bf16)...]
where the time goes in v4:
time: 107 us
  Pallas kernels  106 us (99%)
  local copies, waits for them, and re-layouts  1.67 us (2%)
    pallas_call x1, Pallas kernels, body(): pl.pallas_call(kernel, out_shape=jax.ShapeDtypeStruct((ROWS, COLS), bf16)...  106 us

profile of v4, /device:TPU:1, one launch (start us, length us, event | category | flops | bytes accessed | tf_op | source)
XLA Modules:
  0.0 107.3 jit_solution(7801231260655084896)
XLA Ops:
  0.0 0.0 copy-start
  0.0 1.0 copy-done
  1.0 105.6 %newton_schulz.1 = bf16[224,576]{1,0:T(8,128)(2,1)S(1)} custom-call(bf16[224,576]{1,0:T(8,128)(2,1)S(1)} %copy-done), custom_call_target="tpu_custom_call" | custom-call | flops 2774532096 | bytes 516096 | tf_op jit(solution)/shard_map/newton_schulz/pallas_call | solution.py:455
  106.5 0.7 copy.3
Async XLA Ops:
  0.0 1.0 copy-start

commit v5 on v4

--- a/solution.py
+++ b/solution.py
@@ -27,6 +27,7 @@
 FIRST = pl.ds(0, 256)
 STRIP = 128
 SECOND = pl.ds(256, COLS - 256)
+SPLIT = (pl.ds(0, 128), pl.ds(128, COLS - 384))
 NT = (((1,), (1,)), ((), ()))
 
 
@@ -200,19 +201,37 @@
             near_send.at[g, k], near_recv.at[g, k], along(near[k]),
         )
 
-    def far_copy(g, k):
-        piece = pl.ds(pl.multiple_of(((a + k + 1) % 4) * PIECE, PIECE), PIECE)
-        return remote(
-            far_out.at[piece, half(g)], far_in.at[k, :, half(g)],
+    def piece_of(d):
+        return (a + d + 4 + r + 2 * c) % 4
+
+    def rows_in(i, size=PIECE):
+        return pl.ds(pl.multiple_of(i * PIECE, PIECE), size)
+
+    def sized(i, act):
+        @pl.when(i == 3)
+        def _():
+            act(PIECE // 2)
+
+        @pl.when(i != 3)
+        def _():
+            act(PIECE)
+
+    def far_copy(g, k, size):
+        return remote(
+            far_out.at[rows_in(piece_of(k + 1), size), half(g)],
+            far_in.at[k, pl.ds(0, size), half(g)],
             far_send.at[g, k], far_recv.at[g, k], along(4 * (k + 1)),
         )
 
-    def mine(k=0):
-        return pl.ds(pl.multiple_of(((a + 4 - k) % 4) * PIECE, PIECE), PIECE)
-
-    def gf_copy(g, k):
-        piece = gram.at[c, r, mine(), half(g)]
+    def mine():
+        return rows_in(piece_of(0))
+
+    def gf_copy(g, k, size):
+        piece = gram.at[c, r, rows_in(piece_of(0), size), half(g)]
         return remote(piece, piece, gf_send.at[g, k], gf_recv.at[g, k], along(4 * (k + 1)))
+
+    def gf_arrived(g, k, size):
+        arrived(gram.at[c, r, rows_in(piece_of(-1 - k), size), half(g)], gf_recv.at[g, k])
 
     def quarter_of(core, q, g):
         return gram.at[core, q, pl.ds(0, PART), half(g)]
@@ -246,19 +265,19 @@
         )
         far_out[:, half(g)] = cls[:, half(g)].astype(bf16)
         for k in (1, 0, 2):
-            far_copy(g, k).start()
+            sized(piece_of(k + 1), lambda n: far_copy(g, k, n).start())
 
     for g in range(2):
         total = cls[mine(), half(g)]
         for k in (0, 2, 1):
-            far_copy(g, k).wait_recv()
+            sized(piece_of(0), lambda n: far_copy(g, k, n).wait_recv())
             total += far_in[k, :, half(g)].astype(f32)
         gram[c, r, mine(), half(g)] = total.astype(bf16)
         for k in (1, 0, 2):
-            gf_copy(g, k).start()
+            sized(piece_of(0), lambda n: gf_copy(g, k, n).start())
     for g in range(2):
         for k in (0, 2, 1):
-            arrived(gram.at[c, r, mine(k + 1), half(g)], gf_recv.at[g, k])
+            sized(piece_of(-1 - k), lambda n: gf_arrived(g, k, n))
         for k in (2, 0, 1):
             gn_copy(g, k).start()
         hand(g, 0).start()
@@ -279,11 +298,14 @@
     def dot(left, right):
         return jnp.dot(left, right, preferred_element_type=f32)
 
-    def tx_copy(g, k):
-        return remote(
-            tx_out.at[k, share(g)], tx_in.at[k, share(g)],
-            tx_send.at[g, k], tx_recv.at[g, k], on_x(k),
-        )
+    def tx_copy(g, n, k):
+        return remote(
+            tx_out.at[k, share(g), SPLIT[n]], tx_in.at[k, share(g), SPLIT[n]],
+            tx_send.at[g, n, k], tx_recv.at[g, n, k], on_x(k),
+        )
+
+    def second(n):
+        return pl.ds(SECOND.start + SPLIT[n].start, SPLIT[n].size)
 
     def strip(f):
         return pl.ds(f * STRIP, STRIP)
@@ -308,33 +330,35 @@
                     ).astype(bf16)
                     ty_copy(f, k).start()
         gram_t[half(g)] = gram[:, :, 0:PART, half(g)].reshape(BLOCK, HALVES[g][1]).T
-        for k in (2, 1, 3):
-            tx_out[k, share(g)] = dot(gram_t[rows_of(g, (x + k) % SIDE)], xi[:, SECOND]).astype(
-                bf16
-            )
-            tx_copy(g, k).start()
+        for n in range(2):
+            for k in (2, 1, 3):
+                tx_out[k, share(g), SPLIT[n]] = dot(
+                    gram_t[rows_of(g, (x + k) % SIDE)], xi[:, second(n)]
+                ).astype(bf16)
+                tx_copy(g, n, k).start()
         tx_sum[share(g)] = dot(gram_t[rows_of(g, x)], xi[:, SECOND])
 
-    def ux_copy(g, k):
-        here = ux.at[rows_of(g, x)]
-        return remote(here, here, ux_send.at[g, k], ux_recv.at[g, k], on_x(k))
+    def ux_copy(g, n, k):
+        here = ux.at[rows_of(g, x), SPLIT[n]]
+        return remote(here, here, ux_send.at[g, n, k], ux_recv.at[g, n, k], on_x(k))
 
     def uy_copy(f, k):
         here = uy.at[rows_at(y), strip(f)]
         return remote(here, here, uy_send.at[f, k], uy_recv.at[f, k], on_y(k))
 
-    def ux_part(g):
-        total = tx_sum[share(g)]
+    def ux_part(g, n):
+        total = tx_sum[share(g), SPLIT[n]]
         for k in (1, 3, 2):
-            tx_copy(g, k).wait_recv()
-            total += tx_in[k, share(g)].astype(f32)
-        ux[rows_of(g, x)] = (
-            coef_quad * xj[rows_of(g, x), SECOND].astype(f32) + coef_cubic * total
+            tx_copy(g, n, k).wait_recv()
+            total += tx_in[k, share(g), SPLIT[n]].astype(f32)
+        ux[rows_of(g, x), SPLIT[n]] = (
+            coef_quad * xj[rows_of(g, x), second(n)].astype(f32) + coef_cubic * total
         ).astype(bf16)
         for k in (2, 1, 3):
-            ux_copy(g, k).start()
-
-    ux_part(0)
+            ux_copy(g, n, k).start()
+
+    ux_part(0, 0)
+    ux_part(0, 1)
     for f in range(2):
         total = dot(gram_rows(y), xj[:, strip(f)])
         for k in (1, 3, 2):
@@ -345,7 +369,7 @@
         ).astype(bf16)
         for k in (2, 1, 3):
             uy_copy(f, k).start()
-    ux_part(1)
+        ux_part(1, f)
 
     def px_copy(f, k):
         return remote(
@@ -353,8 +377,11 @@
             px_send.at[f, k], px_recv.at[f, k], on_x(k),
         )
 
-    def py_copy(q):
-        return remote(py_out.at[q], py_in.at[y], py_send.at[q], py_recv.at[y], from_i(q))
+    def py_copy(n, q):
+        return remote(
+            py_out.at[q, :, SPLIT[n]], py_in.at[y, :, SPLIT[n]],
+            py_send.at[n, q], py_recv.at[n, y], from_i(q),
+        )
 
     for f in range(2):
         for k in (1, 3, 2):
@@ -364,20 +391,22 @@
                 gram_t[rows_at((x + k) % SIDE)], uy[:, strip(f)]
             ).astype(bf16)
             px_copy(f, k).start()
-    for g in range(2):
-        for k in (1, 3, 2):
-            arrived(ux.at[rows_of(g, (x + SIDE - k) % SIDE)], ux_recv.at[g, k])
-    for q in range(SIDE):
-        local = jnp.logical_and(own, q == quarter)
-        py_out[q] = dot(gram_rows(q), ux[...]).astype(bf16)
-
-        @pl.when(local)
-        def _():
-            pltpu.make_async_copy(py_out.at[q], py_in.at[y], py_recv.at[y]).start()
-
-        @pl.when(jnp.logical_not(local))
-        def _():
-            py_copy(q).start()
+        for g in range(2):
+            for k in (1, 3, 2):
+                arrived(ux.at[rows_of(g, (x + SIDE - k) % SIDE), SPLIT[f]], ux_recv.at[g, f, k])
+        for q in range(SIDE):
+            local = jnp.logical_and(own, q == quarter)
+            py_out[q, :, SPLIT[f]] = dot(gram_rows(q), ux[:, SPLIT[f]]).astype(bf16)
+
+            @pl.when(local)
+            def _():
+                pltpu.make_async_copy(
+                    py_out.at[q, :, SPLIT[f]], py_in.at[y, :, SPLIT[f]], py_recv.at[f, y]
+                ).start()
+
+            @pl.when(jnp.logical_not(local))
+            def _():
+                py_copy(f, q).start()
 
     factor = math.sqrt(max(M, N))
 
@@ -413,25 +442,27 @@
         s_copy(g).wait_send()
         for k in range(3):
             near_copy(g, k).wait_send()
-            far_copy(g, k).wait_send()
-            gf_copy(g, k).wait_send()
+            sized(piece_of(k + 1), lambda n: far_copy(g, k, n).wait_send())
+            sized(piece_of(0), lambda n: gf_copy(g, k, n).wait_send())
             gn_copy(g, k).wait_send()
         for k in range(4):
             hand(g, k).wait_send()
         for k in (1, 2, 3):
-            tx_copy(g, k).wait_send()
-            ux_copy(g, k).wait_send()
+            for n in range(2):
+                tx_copy(g, n, k).wait_send()
+                ux_copy(g, n, k).wait_send()
     for f in range(2):
         for k in (1, 2, 3):
             ty_copy(f, k).wait_send()
             uy_copy(f, k).wait_send()
             px_copy(f, k).wait_send()
 
-    result = coef_linear * m_ref[:, SECOND].astype(f32)
-    for k in range(SIDE):
-        arrived(py_in.at[k], py_recv.at[k])
-        result += py_in[k].astype(f32)
-    out_ref[:, SECOND] = (result * factor).astype(bf16)
+    for n in range(2):
+        result = coef_linear * m_ref[:, second(n)].astype(f32)
+        for k in range(SIDE):
+            arrived(py_in.at[k, :, SPLIT[n]], py_recv.at[n, k])
+            result += py_in[k, :, SPLIT[n]].astype(f32)
+        out_ref[:, second(n)] = (result * factor).astype(bf16)
 
     @pl.when(others)
     def _():
@@ -440,11 +471,12 @@
             out_ref[:, strip(f)] = fin_in[:, strip(f)]
             fin_copy(f).wait_send()
 
-    for q in range(SIDE):
-
-        @pl.when(jnp.logical_not(jnp.logical_and(own, q == quarter)))
-        def _():
-            py_copy(q).wait_send()
+    for n in range(2):
+        for q in range(SIDE):
+
+            @pl.when(jnp.logical_not(jnp.logical_and(own, q == quarter)))
+            def _():
+                py_copy(n, q).wait_send()
 
 
 def body(momentum):
@@ -493,12 +525,12 @@
             sem((2, 3)), sem((2, 3)),
             sem((2, 4)), sem((2, 4)),
             sem((1,)), sem((1,)),
+            sem((2, 2, SIDE)), sem((2, 2, SIDE)),
+            sem((2, SIDE)), sem((2, SIDE)),
+            sem((2, 2, SIDE)), sem((2, 2, SIDE)),
             sem((2, SIDE)), sem((2, SIDE)),
             sem((2, SIDE)), sem((2, SIDE)),
             sem((2, SIDE)), sem((2, SIDE)),
-            sem((2, SIDE)), sem((2, SIDE)),
-            sem((2, SIDE)), sem((2, SIDE)),
-            sem((SIDE,)), sem((SIDE,)),
             sem((2,)), sem((2,)),
             pltpu.SemaphoreType.REGULAR((2,)),
         ],

time: 107 us -> 105 us (0.981)
  Pallas kernels: 106 us -> 104 us
    pallas_call x1, Pallas kernels: 106 us -> 104 us  [body(): pl.pallas_call(kernel, out_shape=jax.ShapeDtypeStruct((ROWS, COLS), bf16)...]
where the time goes in v5:
time: 105 us
  Pallas kernels  104 us (99%)
  local copies, waits for them, and re-layouts  1.67 us (2%)
    pallas_call x1, Pallas kernels, body(): pl.pallas_call(kernel, out_shape=jax.ShapeDtypeStruct((ROWS, COLS), bf16)...  104 us

profile of v5, /device:TPU:1, one launch (start us, length us, event | category | flops | bytes accessed | tf_op | source)
XLA Modules:
  0.0 105.2 jit_solution(9187639738861758584)
XLA Ops:
  0.0 0.0 copy-start
  0.0 1.0 copy-done
  1.0 103.5 %newton_schulz.1 = bf16[224,576]{1,0:T(8,128)(2,1)S(1)} custom-call(bf16[224,576]{1,0:T(8,128)(2,1)S(1)} %copy-done), custom_call_target="tpu_custom_call" | custom-call | flops 2774532096 | bytes 516096 | tf_op jit(solution)/shard_map/newton_schulz/pallas_call | solution.py:487
  104.5 0.7 copy.3
Async XLA Ops:
  0.0 1.0 copy-start

commit v6 on v5

--- a/solution.py
+++ b/solution.py
@@ -142,6 +142,8 @@
     def _():
         for k in (2, 1, 3):
             j_copy(m_ref, k).start()
+        for k in (1, 3):
+            i_copy(k).start()
         keep(m_ref)
 
     @pl.when(others)
@@ -158,9 +160,8 @@
     def _():
         for k in (2, 1, 3):
             j_copy(swap, k).start()
-
-    for k in (1, 3):
-        i_copy(k).start()
+        for k in (1, 3):
+            i_copy(k).start()
 
     @pl.when(others)
     def _():

time: 105 us -> 104 us (level)
  Pallas kernels: 104 us -> 102 us
    pallas_call x1, Pallas kernels: 104 us -> 102 us  [body(): pl.pallas_call(kernel, out_shape=jax.ShapeDtypeStruct((ROWS, COLS), bf16)...]
where the time goes in v6:
time: 104 us
  Pallas kernels  102 us (98%)
  local copies, waits for them, and re-layouts  1.67 us (2%)
    pallas_call x1, Pallas kernels, body(): pl.pallas_call(kernel, out_shape=jax.ShapeDtypeStruct((ROWS, COLS), bf16)...  102 us

profile of v6, /device:TPU:1, one launch (start us, length us, event | category | flops | bytes accessed | tf_op | source)
XLA Modules:
  0.0 104.1 jit_solution(15019602633994104839)
XLA Ops:
  0.0 0.0 copy-start
  0.0 1.0 copy-done
  1.0 102.5 %newton_schulz.1 = bf16[224,576]{1,0:T(8,128)(2,1)S(1)} custom-call(bf16[224,576]{1,0:T(8,128)(2,1)S(1)} %copy-done), custom_call_target="tpu_custom_call" | custom-call | flops 2774532096 | bytes 516096 | tf_op jit(solution)/shard_map/newton_schulz/pallas_call | solution.py:488
  103.4 0.7 copy.3
Async XLA Ops:
  0.0 1.0 copy-start
